TPU v7x, 32 devices: a whole 2x2x4 slice. The times are simulated.
32 devices in a mesh: depth: 8 (over z, x), batch: 4 (over y, core).
Axes of the slice: x: 2, y: 2, z: 4, core: 2. Of those that a mesh axis runs over, the one named last changes fastest.
Arguments:
- cpoint_guess: float32 [8, 4, 32, 4096], P('depth', 'batch'), may hold values from -6 to 6
- adjoint_guess: float32 [8, 4, 32, 4096], P('depth', 'batch'), may hold values from -6 to 6
- weights: float32 [64, 32, 32], P('depth'), may hold values from -0.5 to 0.5
- biases: float32 [64, 32], P('depth'), may hold values from -3 to 3
- diffusion: float32 [32], replicated, may hold values from 0.02 to 0.25
- section_len: int32 [8], replicated, may hold values from 1 to 8, 24 in all
Outputs:
- states_out: float32 [8, 4, 32, 4096], P('depth', 'batch')
- adjoint_out: float32 [8, 4, 32, 4096], P('depth', 'batch')
- grad_weights: float32 [64, 32, 32], P('depth')
- grad_biases: float32 [64, 32], P('depth')
Inputs may be any that keep to these rules, and one draw needn't show every extreme that they name: `section_len`: each of the 8 sections holds 1 to 8 layers, 24 in all, and one section holds exactly 8.
All inputs are finite; a program needn't handle non-finite values.
Results may differ from a plain program's by a relative error of at most 0.0003.
Values sent between devices are 32-bit elements; how exact they have to be, the bound alone decides.
No kernel may reach another device: no remote copies, remote signals or barrier semaphores. Data moves between devices by JAX's collectives and lax.ppermute only.
A program may use at most 128 MiB of HBM per device.

v0:
```python
import functools

import jax
import jax.numpy as jnp
from jax import lax
from jax.experimental import pallas as pl
from jax.experimental.pallas import tpu as pltpu
from jax.sharding import PartitionSpec as P

IMG = 64
LANES = 128
CHUNK = 256
AT_ONCE = 4
F32 = jnp.float32
BF16 = jnp.bfloat16


def split(x):
    hi = x.astype(BF16)
    lo = (x - hi.astype(F32)).astype(BF16)
    return hi, lo


def stack3(hi, lo):
    return jnp.concatenate([hi, lo, hi], axis=0)


def left_factor(matrix):
    hi = matrix.astype(BF16).astype(F32)
    return jnp.concatenate([hi, hi, matrix - hi], axis=1).astype(BF16)


def mm(a, b):
    return jnp.dot(a, b, preferred_element_type=F32)


def mm_nt(a, b):
    return lax.dot_general(a, b, (((1,), (1,)), ((), ())), preferred_element_type=F32)


def lane_masks(rows):
    lane = lax.broadcasted_iota(jnp.int32, (rows, LANES), 1)
    col = lane % IMG
    return col > 0, col < IMG - 1, lane < IMG


def neighbours(left, mid, right, masks):
    not_first, not_last, upper = masks
    pieces = [left] + [mid[:, k : k + LANES] for k in range(0, mid.shape[1], LANES)] + [right]
    swapped = [pltpu.roll(piece, IMG, 1) for piece in pieces]
    sums = []
    for k in range(1, len(pieces) - 1):
        piece = pieces[k]
        beside = jnp.where(not_first, pltpu.roll(piece, 1, 1), 0.0)
        beside += jnp.where(not_last, pltpu.roll(piece, LANES - 1, 1), 0.0)
        beside += swapped[k] + jnp.where(upper, swapped[k - 1], swapped[k + 1])
        sums.append(beside)
    return jnp.concatenate(sums, axis=1)


def sweep(buf, width, step):
    rows = buf.shape[0]
    masks = lane_masks(rows)
    before = buf[:, 0:LANES]
    for start in range(0, width, CHUNK):
        size = min(CHUNK, width - start)
        at = LANES + start
        mid = buf[:, at : at + size]
        after = buf[:, at + size : at + size + LANES]
        around = neighbours(before, mid, after, masks)
        before = mid[:, size - LANES :]
        buf[:, at : at + size] = step(start, size, mid, around)


def matrix_of(p_ref, slot):
    rows = p_ref.shape[0]
    return p_ref[:, slot * rows : (slot + 1) * rows]


def table_of(p_ref):
    return p_ref[:, p_ref.shape[1] - LANES :]


def bias_of(p_ref, slot):
    table = table_of(p_ref)
    pick = lax.broadcasted_iota(jnp.int32, table.shape, 1) == slot
    return jnp.sum(jnp.where(pick, table, 0.0), axis=1, keepdims=True)


def slots_of(p_ref):
    rows, width = p_ref.shape
    return (width - LANES) // rows


def prepare(p_ref, wl_ref, wt_ref):
    most = slots_of(p_ref)
    factor = 1.0 / most
    for slot in range(most):
        matrix = matrix_of(p_ref, slot)
        wl_ref[slot] = left_factor(matrix)
        wt_ref[slot] = left_factor((factor * matrix).T)
    return factor * table_of(p_ref)[:, most : most + 1], factor


def column(row):
    n = row.shape[1]
    same = lax.broadcasted_iota(jnp.int32, (n, n), 0) == lax.broadcasted_iota(jnp.int32, (n, n), 1)
    return jnp.sum(jnp.where(same, row, 0.0), axis=1, keepdims=True)


def length_of(p_ref, section):
    row = table_of(p_ref)[0:1, :]
    pick = lax.broadcasted_iota(jnp.int32, row.shape, 1) == slots_of(p_ref) + 1 + section
    return jnp.sum(jnp.where(pick, row, 0.0)).astype(jnp.int32)


def pack_kernel(
    w_any, b_any, diff_any, len_any, guess_any, p_ref, p0_ref, both_ref, w_ref, b_ref, diff_ref, len_ref, sem
):
    most, rows, _ = w_ref.shape
    width = guess_any.shape[1]
    copies = [
        pltpu.make_async_copy(source, target, sem.at[k])
        for k, (source, target) in enumerate(
            [(w_any, w_ref), (b_any, b_ref), (diff_any, diff_ref), (len_any, len_ref),
             (guess_any, both_ref.at[:, 0:width])]
        )
    ]
    for copy in copies:
        copy.start()
    for copy in copies[:-1]:
        copy.wait()
    wide = most * rows
    p_ref[:, wide:] = jnp.zeros((rows, LANES), F32)
    for slot in range(most):
        p_ref[:, slot * rows : (slot + 1) * rows] = w_ref[slot]
        p_ref[:, wide + slot : wide + slot + 1] = column(b_ref[slot : slot + 1, :])
    p_ref[:, wide + most : wide + most + 1] = column(diff_ref[...])
    lengths = len_ref[...].astype(F32)
    first = wide + most + 1
    p_ref[:, first : first + lengths.shape[1]] = jnp.broadcast_to(lengths, (rows, lengths.shape[1]))
    p0_ref[...] = jnp.zeros_like(p0_ref)
    p0_ref[:, 0:rows] = w_ref[0]
    p0_ref[:, rows : rows + 1] = column(b_ref[0:1, :])
    both_ref[:, width:] = p_ref[...]
    copies[-1].wait()


def forward_layer(buf, width, wl, wt, bias, spread, t_out=None, u_out=None):
    keep = 1.0 - 4.0 * spread

    def step(start, size, mid, around):
        hi, lo = split(mid)
        t_hi, t_lo = split(jnp.tanh(mm(wl, stack3(hi, lo)) + bias))
        if t_out is not None:
            t_out(start, size, t_hi, t_lo)
        if u_out is not None:
            u_out(start, size, hi, lo)
        return mid * keep + around * spread - mm(wt, stack3(t_hi, t_lo))

    sweep(buf, width, step)


def run_forward(buf, width, p_ref, wl_ref, wt_ref, spread, count, t_refs=None, u_refs=None):
    def saver(refs, slot):
        if refs is None:
            return None

        def save(start, size, hi, lo):
            refs[0][slot, :, start : start + size] = hi
            refs[1][slot, :, start : start + size] = lo

        return save

    @pl.loop(0, count)
    def _(slot):
        forward_layer(
            buf, width, wl_ref[slot], wt_ref[slot], bias_of(p_ref, slot), spread,
            saver(t_refs, slot), saver(u_refs, slot),
        )


def run_backward(buf, width, wl_ref, wt_ref, spread, count, t_refs, u_refs=None, grads=None):
    keep = 1.0 - 4.0 * spread

    @pl.loop(0, count)
    def _(passed):
        slot = count - 1 - passed
        wl, wt = wl_ref[slot], wt_ref[slot]
        rows = buf.shape[0]
        sums = []

        def step(start, size, mid, around):
            span = slice(start, start + size)
            hi, lo = split(mid)
            t = t_refs[0][slot, :, span].astype(F32) + t_refs[1][slot, :, span].astype(F32)
            q = (1.0 - t * t) * mm(wl, stack3(hi, lo))
            q_hi, q_lo = split(q)
            if grads is not None:
                _, _, lam_ref, q_ref = grads
                lam_ref[0:rows, span], lam_ref[rows:, span] = hi, lo
                q_ref[0:rows, span], q_ref[rows:, span] = q_hi, q_lo
                sums.append(sum(q[:, k : k + LANES] for k in range(0, size, LANES)))
            return mid * keep + around * spread - mm(wt, stack3(q_hi, q_lo))

        sweep(buf, width, step)
        if grads is not None:
            g_ref, factor, lam_ref, q_ref = grads

            def product(left, right):
                g = mm_nt(left, right)
                return g[:rows, :rows] + g[:rows, rows:] + g[rows:, :rows]

            gw = product(jnp.concatenate([ref[slot] for ref in t_refs], axis=0), lam_ref[...])
            gw += product(q_ref[...], jnp.concatenate([ref[slot] for ref in u_refs], axis=0))
            g_ref[slot, :, 0:rows] = -factor * gw
            g_ref[slot, :, rows : rows + 1] = -factor * jnp.sum(sum(sums), axis=1, keepdims=True)


def fill(buf, value):
    rows, width = value.shape
    zero = jnp.zeros((rows, LANES), F32)
    buf[:, 0:LANES] = zero
    buf[:, LANES + width :] = zero
    buf[:, LANES : LANES + width] = value


def inner(buf):
    return buf[:, LANES : buf.shape[1] - LANES]


class Plan:
    def __init__(self, count):
        self.count = count
        self.items = count - 2
        self.hosts = count // 2
        self.first = count // 4
        self.block = IMG // self.hosts
        self.rows = min(IMG, self.block + 2 * (count - 4))
        self.rows += self.rows % 2
        self.results = count - 3
        self.local = (self.first - 3) % self.results

    def window(self, host):
        start = host * self.block - (self.count - 4)
        return jnp.clip(start - start % 2, 0, IMG - self.rows)

    def in_pairs(self, shift):
        return [((h + shift) % self.items, h + self.first) for h in range(self.hosts)]

    def out_pairs(self, shift):
        pairs = [(h + self.first, 3 + (h + shift) % self.results) for h in range(self.hosts)]
        pairs = [(s, d) for s, d in pairs if s != d]
        return pairs + ([(0, 2)] if shift < self.hosts else [])


def lanes(row, size):
    return pl.ds(pl.multiple_of(row * IMG, LANES), size * IMG)


def push_kernel(both_ref, out_ref, buf, wl, wt):
    width = out_ref.shape[1]
    p_ref = both_ref.at[:, width:]
    spread, _ = prepare(p_ref, wl, wt)
    fill(buf, both_ref[:, 0:width])
    run_forward(buf, width, p_ref, wl, wt, spread, length_of(p_ref, lax.axis_index("depth")))
    out_ref[...] = inner(buf)


def tau_kernel(plan, point_ref, p_ref, p2_ref, second_ref, *rest):
    msgs, (buf, wl, wt, whole) = rest[:-4], rest[-4:]
    rows, width = point_ref.shape
    own = lax.axis_index("depth")
    count = length_of(p_ref, jnp.minimum(own + 1, plan.count - 1))
    spread, factor = prepare(p_ref, wl, wt)
    fill(buf, point_ref[...])
    run_forward(buf, width, p_ref, wl, wt, spread, count)
    second_ref[...] = inner(buf)

    def coarse(matrix, bias, length):
        scale = length.astype(F32)
        forward_layer(
            buf, width, left_factor(matrix), left_factor((scale * factor * matrix).T), bias, scale * spread
        )

    @pl.when(own > 0)
    def _():
        buf[:, LANES : LANES + width] = point_ref[...]
        coarse(matrix_of(p_ref, 0), bias_of(p_ref, 0), count)
        whole[...] = second_ref[...] - inner(buf)

    @pl.when(own == 0)
    def _():
        coarse(p2_ref[:, 0:rows], p2_ref[:, rows : rows + 1], length_of(p_ref, 2))
        whole[...] = inner(buf)

    size = plan.rows * IMG
    bias = bias_of(p_ref, 0)
    for shift, msg in enumerate(msgs):
        host = lax.rem(own - shift + 2 * plan.items, plan.items)
        start = plan.window(jnp.minimum(host, plan.hosts - 1))
        msg[:, 0:size] = whole[:, lanes(start, plan.rows)]
        msg[:, size : size + rows] = matrix_of(p_ref, 0)
        msg[:, size + rows : size + rows + 1] = bias


def point_kernel(_, both_ref, before_ref, adj_ref, point_ref, lam_ref, t_hi, t_lo, u_hi, u_lo, buf, wl, wt):
    own = lax.axis_index("depth")
    width = point_ref.shape[1]

    @pl.when(own > 0)
    def _():
        p_before_ref = before_ref.at[:, width:]
        count = length_of(p_before_ref, jnp.maximum(own - 1, 0))
        spread, _ = prepare(p_before_ref, wl, wt)
        fill(buf, before_ref[:, 0:width])
        run_forward(buf, width, p_before_ref, wl, wt, spread, count)
        point_ref[...] = inner(buf)

    @pl.when(own == 0)
    def _():
        point_ref[...] = both_ref[:, 0:width]
        fill(buf, both_ref[:, 0:width])

    p_ref = both_ref.at[:, width:]
    count = length_of(p_ref, own)
    spread, _ = prepare(p_ref, wl, wt)
    run_forward(buf, width, p_ref, wl, wt, spread, count, (t_hi, t_lo), (u_hi, u_lo))

    @pl.when(own > 0)
    def _():
        fill(buf, adj_ref[...])
        run_backward(buf, width, wl, wt, spread, count, (t_hi, t_lo))
        lam_ref[...] = inner(buf)


def adjoint_kernel(
    _, adj_ref, lam_after_ref, p_ref, t_hi, t_lo, u_hi, u_lo, adj_out_ref, g_ref, buf, wl, wt, lam_ref, q_ref, g_all
):
    own = lax.axis_index("depth")
    last = lax.axis_size("depth") - 1
    rows, width = adj_out_ref.shape
    g_all[...] = jnp.zeros_like(g_all)

    @pl.when(own < last)
    def _():
        fill(buf, lam_after_ref[...])

    @pl.when(own == last)
    def _():
        fill(buf, adj_ref[...])

    spread, factor = prepare(p_ref, wl, wt)
    run_backward(
        buf, width, wl, wt, spread, length_of(p_ref, own), (t_hi, t_lo), (u_hi, u_lo),
        (g_all, factor, lam_ref, q_ref),
    )
    adj_out_ref[...] = inner(buf)
    most = g_all.shape[0]
    g_ref[:, most * rows :] = jnp.zeros((rows, LANES), F32)
    for slot in range(most):
        g_ref[:, slot * rows : (slot + 1) * rows] = g_all[slot, :, 0:rows]
        g_ref[:, most * rows + slot : most * rows + slot + 1] = g_all[slot, :, rows : rows + 1]


def sum_kernel(*refs):
    parts, (gw_ref, gb_ref) = refs[:-2], refs[-2:]
    most, rows, _ = gw_ref.shape
    total = sum(part[...] for part in parts)
    for slot in range(most):
        gw_ref[slot] = total[:, slot * rows : (slot + 1) * rows]
    gb_ref[...] = total[:, most * rows :].T[:most, :]


def chain_kernel(plan, _, second_ref, p_ref, *rest):
    msgs, rest = rest[: plan.items], rest[plan.items :]
    outs, (buf, held, done, wl, wt, sem) = rest[: plan.results], rest[plan.results :]
    own = lax.axis_index("depth")
    host = own - plan.first
    rows = held.shape[1]
    size = plan.rows * IMG
    piece = plan.block * IMG

    @pl.when(jnp.logical_and(host >= 0, host < plan.hosts))
    def _():
        copies = [
            pltpu.make_async_copy(msg, held.at[lax.rem(host + shift, plan.items)], sem.at[shift])
            for shift, msg in enumerate(msgs)
        ]
        for copy in copies:
            copy.start()
        for copy in copies:
            copy.wait()
        offset = host * plan.block - plan.window(host)
        most = slots_of(p_ref)
        spread = table_of(p_ref)[:, most : most + 1] * (1.0 / most)
        for item in range(2, plan.items):
            matrix = held[item, :, size : size + rows]
            scale = length_of(p_ref, item + 1).astype(F32) * (1.0 / most)
            wl[item] = left_factor(matrix)
            wt[item] = left_factor((scale * matrix).T)
        fill(buf, held[0, :, 0:size] + held[1, :, 0:size])

        def keep(result):
            done[result] = buf[:, pl.ds(pl.multiple_of(LANES + offset * IMG, LANES), piece)]

        keep(0)

        @pl.loop(2, plan.items)
        def _(item):
            forward_layer(
                buf, size, wl[item], wt[item], held[item, :, size + rows : size + rows + 1],
                length_of(p_ref, item + 1).astype(F32) * spread,
            )
            buf[:, LANES : LANES + size] = inner(buf) + held[item, :, 0:size]
            keep(item - 1)

        for shift, out in enumerate(outs):
            out[...] = done[lax.rem(host + shift, plan.results)]

    @pl.when(own == 0)
    def _():
        for shift, out in enumerate(outs):
            if shift < plan.hosts:
                out[...] = second_ref[:, shift * piece : (shift + 1) * piece]


def collect_kernel(plan, point_ref, local_ref, *rest):
    received, out_ref = rest[:-1], rest[-1]
    own = lax.axis_index("depth")
    host = own - plan.first

    @pl.when(own < 2)
    def _():
        out_ref[...] = point_ref[...]

    @pl.when(own == 2)
    def _():
        for shift, block in enumerate(received):
            if shift < plan.hosts:
                out_ref[:, lanes(shift * plan.block, plan.block)] = block[...]

    for shift, block in enumerate(received):
        sender = lax.rem(own - 3 - shift + 2 * plan.results, plan.results)

        @pl.when(jnp.logical_and(own > 2, jnp.logical_and(sender < plan.hosts, sender != host)))
        def _():
            out_ref[:, lanes(sender * plan.block, plan.block)] = block[...]

    @pl.when(jnp.logical_and(own > 2, jnp.logical_and(host >= 0, host < plan.hosts)))
    def _():
        out_ref[:, lanes(host * plan.block, plan.block)] = local_ref[...]


SMEM = pl.BlockSpec(memory_space=pltpu.SMEM)
VMEM = pl.BlockSpec(memory_space=pltpu.VMEM)
ANY = pl.BlockSpec(memory_space=pl.ANY)


def call(kernel, out_shape, in_specs, scratch, micros, name, mebi=32):
    return pl.pallas_call(
        kernel,
        out_shape=out_shape,
        in_specs=in_specs,
        out_specs=jax.tree.map(lambda _: VMEM, out_shape),
        scratch_shapes=scratch,
        compiler_params=pltpu.CompilerParams(vmem_limit_bytes=mebi * 2**20),
        cost_estimate=pl.CostEstimate(flops=int(micros * 1e8), bytes_accessed=2**21, transcendentals=0),
        name=name,
    )


def shifted(value, steps):
    count = lax.axis_size("depth")
    first, end = max(0, -steps), min(count, count - steps)
    return lax.ppermute(value, "depth", [(s, s + steps) for s in range(first, end)])


def others(value, step):
    count = lax.axis_size("batch")
    xor = count & (count - 1) == 0
    return lax.ppermute(value, "batch", [(s, s ^ step if xor else (s + step) % count) for s in range(count)])


def body(cpoint_guess, adjoint_guess, weights, biases, diffusion, section_len):
    plan = Plan(lax.axis_size("depth"))
    most, rows, _ = weights.shape
    width = cpoint_guess.shape[-1]
    guess, adjoint = cpoint_guess[0, 0], adjoint_guess[0, 0]

    def shape(*dims):
        return jax.ShapeDtypeStruct(dims, F32)

    state = shape(rows, width)
    buffer = pltpu.VMEM((rows, width + 2 * LANES), F32)
    factors = [pltpu.VMEM((most, rows, 3 * rows), BF16)] * 2

    wide = most * rows + LANES
    packed, packed0, both = call(
        pack_kernel, [shape(rows, wide), shape(rows, LANES), shape(rows, width + wide)], [ANY] * 5,
        [
            pltpu.VMEM(weights.shape, F32), pltpu.VMEM(biases.shape, F32), pltpu.VMEM((1, rows), F32),
            pltpu.VMEM((1, plan.count), jnp.int32), pltpu.SemaphoreType.DMA((5,)),
        ],
        1, "pack", 60,
    )(weights, biases, diffusion[None], section_len[None], guess)
    packed_after = shifted(packed, -1)
    packed_second = lax.ppermute(packed0, "depth", [(2, 0)])
    before = shifted(both, 1)
    after = call(push_kernel, state, [VMEM], [buffer, *factors], 40, "push")(both)
    after, packed_after, packed_second = lax.optimization_barrier((after, packed_after, packed_second))

    saved = jax.ShapeDtypeStruct((most, rows, width), BF16)
    window = shape(rows, plan.rows * IMG + LANES)
    second, *msgs = call(
        functools.partial(tau_kernel, plan), [state] + [window] * plan.items,
        [VMEM] * 3, [buffer, *factors, pltpu.VMEM((rows, width), F32)], 3, "tau",
    )(after, packed_after, packed_second)
    arrived = {plan.first: msgs[plan.first]}
    order = [shift for shift in range(plan.items) if shift != plan.first]
    for k, shift in enumerate(order):
        msg = msgs[shift]
        if k >= AT_ONCE:
            msg, _ = lax.optimization_barrier((msg, arrived[order[k - AT_ONCE]]))
        arrived[shift] = lax.ppermute(msg, "depth", plan.in_pairs(shift))
    msgs = [arrived[shift] for shift in range(plan.items)]

    point, lam, *kept = call(
        point_kernel, [state] * 2 + [saved] * 4, [ANY] + [VMEM] * 3, [buffer, *factors], 6, "point"
    )(msgs[plan.first], both, before, adjoint)
    lam, msgs = lax.optimization_barrier((lam, msgs))
    lam_after = shifted(lam, -1)

    piece = shape(rows, plan.block * IMG)
    blocks = call(
        functools.partial(chain_kernel, plan), [piece] * plan.results,
        [ANY, VMEM, VMEM] + [ANY] * plan.items,
        [
            pltpu.VMEM((rows, plan.rows * IMG + 2 * LANES), F32),
            pltpu.VMEM((plan.items, *window.shape), F32),
            pltpu.VMEM((plan.results, *piece.shape), F32),
            pltpu.VMEM((plan.items, rows, 3 * rows), BF16),
            pltpu.VMEM((plan.items, rows, 3 * rows), BF16),
            pltpu.SemaphoreType.DMA((plan.items,)),
        ],
        1, "chain",
    )(lam, second, packed, *msgs)
    received = [lax.ppermute(block, "depth", plan.out_pairs(k)) for k, block in enumerate(blocks)]

    pair = pltpu.VMEM((2 * rows, width), BF16)
    adjoint_out, grads = call(
        adjoint_kernel, [state, shape(rows, wide)], [ANY] + [VMEM] * 7,
        [buffer, *factors, pair, pair, pltpu.VMEM((most, rows, rows + 1), F32)], 10, "adjoint",
    )(blocks[plan.local], adjoint, lam_after, packed, *kept)

    states = call(
        functools.partial(collect_kernel, plan), state, [VMEM] * (2 + plan.results), [], 0.5, "collect"
    )(point, blocks[plan.local], *received)
    grads, *_ = lax.optimization_barrier((grads, *received))
    parts = [grads] + [others(grads, step) for step in range(1, lax.axis_size("batch"))]
    gw, gb = call(
        sum_kernel, [shape(*weights.shape), shape(*biases.shape)], [VMEM] * len(parts), [], 0.5, "sum"
    )(*parts)
    return states[None, None], adjoint_out[None, None], gw, gb


def solution(mesh):
    state = P("depth", "batch", None, None)
    return jax.shard_map(
        body,
        mesh=mesh,
        in_specs=(state, state, P("depth", None, None), P("depth", None), P(), P()),
        out_specs=(state, state, P("depth", None, None), P("depth", None)),
        check_vma=False,
    )
```

profile of v0, /device:TPU:0, one launch (start us, length us, event | category | flops | bytes accessed | tf_op | source)
XLA Modules:
  0.0 77.1 jit_solution(8609678281981082012)
XLA Ops:
  0.6 2.1 %pack.1 = (f32[32,384]{1,0:T(8,128)}, f32[32,128]{1,0:T(8,128)}, f32[32,4480]{1,0:T(8,128)}) custom-call(f32[8,32,32]{2,1,0:T(8,128)} %w_any.1, f32[8,32]{1,0:T(8,128)} %b_any.1, f32[1,32]{1,0:T(1,128)} %bitcast.10, s32[1,8]{1,0:T(1,128)} %bitcast.11, f32[32,4096]{1,0:T(8,128)} %bitcast.9), custom_call_target="tpu_custom_call" | custom-call | flops 100000000 | bytes 2097152 | tf_op jit(solution)/shard_map/pack/pallas_call | solution.py:499
  2.7 1.3 %collective-permute-start.1 = (f32[32,128]{1,0:T(8,128)}, f32[32,128]{1,0:T(8,128)S(1)}, u32[]{:S(2)}, u32[]{:S(2)}) collective-permute-start(f32[32,128]{1,0:T(8,128)} %get-tuple-element.43), channel_id=1, source_target_pairs={{8,0},{9,1},{10,2},{11,3}} | collective-permute-start | bytes 49160 | tf_op jit(solution)/shard_map/ppermute | solution.py:508
  4.0 1.3 %collective-permute-start = (f32[32,384]{1,0:T(8,128)}, f32[32,384]{1,0:T(8,128)S(1)}, u32[]{:S(2)}, u32[]{:S(2)}) collective-permute-start(f32[32,384]{1,0:T(8,128)} %get-tuple-element.42.p_ref), channel_id=1, source_target_pairs={{4,0},{8,4},{12,8},{16,12},{20,16},{24,20},{28,24},{5,1},{9,5},{13... | collective-permute-start | bytes 147464 | tf_op jit(solution)/shard_map/ppermute | solution.py:476
  5.4 5.0 %collective-permute-start.2 = (f32[32,4480]{1,0:T(8,128)}, f32[32,4480]{1,0:T(8,128)S(1)}, u32[]{:S(2)}, u32[]{:S(2)}) collective-permute-start(f32[32,4480]{1,0:T(8,128)} %get-tuple-element.41.both_ref), channel_id=1, source_target_pairs={{0,4},{4,8},{8,12},{12,16},{16,20},{20,24},{24,28},{1,5},{5,9},{9,... | collective-permute-start | bytes 1720328 | tf_op jit(solution)/shard_map/ppermute | solution.py:476
  10.4 1.1 %copy-done.2 = f32[32,4480]{1,0:T(8,128)S(1)} copy-done((f32[32,4480]{1,0:T(8,128)S(1)}, f32[32,4480]{1,0:T(8,128)}, u32[]{:S(2)}) %copy-start.2) | copy-done | bytes 573464
  11.4 5.6 %push.1.point_ref = f32[32,4096]{1,0:T(8,128)S(1)} custom-call(f32[32,4480]{1,0:T(8,128)S(1)} %copy-done.2), custom_call_target="tpu_custom_call" | custom-call | flops 4000000000 | bytes 2097152 | tf_op jit(solution)/shard_map/push/pallas_call | solution.py:510
  17.1 2.1 %tau.1 = (f32[32,4096]{1,0:T(8,128)S(1)}, f32[32,1664]{1,0:T(8,128)S(1)}, f32[32,1664]{1,0:T(8,128)S(1)}, f32[32,1664]{1,0:T(8,128)S(1)}, f32[32,1664]{1,0:T(8,1...) custom-call(f32[32,4096]{1,0:T(8,128)S(1)} %push.1.point_ref, f32[32,384]{1,0:T(8,128)S(1)} %collective-permute-done.p_ref, ...), custom_call_target="tpu_custom_call" | custom-call | flops 300000000 | bytes 2097152 | tf_op jit(solution)/shard_map/tau/pallas_call | solution.py:515
  19.2 1.6 %collective-permute-start.3 = (f32[32,1664]{1,0:T(8,128)S(1)}, f32[32,1664]{1,0:T(8,128)S(1)}, u32[]{:S(2)}, u32[]{:S(2)}) collective-permute-start(f32[32,1664]{1,0:T(8,128)S(1)} %get-tuple-element.50), channel_id=1, source_target_pairs={{0,8},{4,12},{8,16},{12,20},{1,9},{5,13},{9,17},{13,21},{2,10},{6,... | collective-permute-start | bytes 638984 | tf_op jit(solution)/shard_map/ppermute | solution.py:525
  20.8 0.7 collective-permute-start.4
  21.4 5.9 %collective-permute-start.5 = (f32[32,1664]{1,0:T(8,128)S(1)}, f32[32,1664]{1,0:T(8,128)S(1)}, u32[]{:S(2)}, u32[]{:S(2)}) collective-permute-start(f32[32,1664]{1,0:T(8,128)S(1)} %get-tuple-element.52), channel_id=1, source_target_pairs={{12,8},{16,12},{20,16},{0,20},{13,9},{17,13},{21,17},{1,21},{14,10... | collective-permute-start | bytes 638984 | tf_op jit(solution)/shard_map/ppermute | solution.py:525
  27.4 5.2 %collective-permute-start.6 = (f32[32,1664]{1,0:T(8,128)S(1)}, f32[32,1664]{1,0:T(8,128)S(1)}, u32[]{:S(2)}, u32[]{:S(2)}) collective-permute-start(f32[32,1664]{1,0:T(8,128)S(1)} %get-tuple-element.53), channel_id=1, source_target_pairs={{16,8},{20,12},{0,16},{4,20},{17,9},{21,13},{1,17},{5,21},{18,10},... | collective-permute-start | bytes 638984 | tf_op jit(solution)/shard_map/ppermute | solution.py:525
  32.6 2.7 %collective-permute-start.7 = (f32[32,1664]{1,0:T(8,128)S(1)}, f32[32,1664]{1,0:T(8,128)S(1)}, u32[]{:S(2)}, u32[]{:S(2)}) collective-permute-start(f32[32,1664]{1,0:T(8,128)S(1)} %get-tuple-element.55), channel_id=1, source_target_pairs={{20,8},{0,12},{4,16},{8,20},{21,9},{1,13},{5,17},{9,21},{22,10},{2... | collective-permute-start | bytes 638984 | tf_op jit(solution)/shard_map/ppermute | solution.py:525
  35.3 5.6 %point.1 = (f32[32,4096]{1,0:T(8,128)S(1)}, f32[32,4096]{1,0:T(8,128)S(1)}, bf16[8,32,4096]{2,1,0:T(8,128)(2,1)S(1)}, bf16[8,32,4096]{2,1,0:T(8,128)(2,1)S(1)}, ...) custom-call(f32[32,1664]{1,0:T(8,128)S(1)} %get-tuple-element.60._.rest_2_, f32[32,4480]{1,0:T(8,128)S(1)} %copy-done.3, ...), custom_call_target="tpu_custom_call" | custom-call | flops 600000000 | bytes 2097152 | tf_op jit(solution)/shard_map/point/pallas_call | solution.py:528
  41.0 1.3 %collective-permute-start.13 = (f32[32,4096]{1,0:T(8,128)S(1)}, f32[32,4096]{1,0:T(8,128)S(1)}, u32[]{:S(2)}, u32[]{:S(2)}) collective-permute-start(f32[32,4096]{1,0:T(8,128)S(1)} %get-tuple-element.56._), channel_id=1, source_target_pairs={{4,0},{8,4},{12,8},{16,12},{20,16},{24,20},{28,24},{5,1},{9,5},{13... | collective-permute-start | bytes 1572872 | tf_op jit(solution)/shard_map/ppermute | solution.py:476
  42.4 10.2 %collective-permute-start.8 = (f32[32,1024]{1,0:T(8,128)S(1)}, f32[32,1024]{1,0:T(8,128)S(1)}, u32[]{:S(2)}, u32[]{:S(2)}) collective-permute-start(f32[32,1024]{1,0:T(8,128)S(1)} %get-tuple-element.65), channel_id=1, source_target_pairs={{8,12},{12,16},{16,20},{20,24},{0,8},{9,13},{13,17},{17,21},{21,25... | collective-permute-start | bytes 393224 | tf_op jit(solution)/shard_map/ppermute | solution.py:548
  52.6 3.1 %collective-permute-start.9 = (f32[32,1024]{1,0:T(8,128)S(1)}, f32[32,1024]{1,0:T(8,128)S(1)}, u32[]{:S(2)}, u32[]{:S(2)}) collective-permute-start(f32[32,1024]{1,0:T(8,128)S(1)} %get-tuple-element.66), channel_id=1, source_target_pairs={{8,16},{12,20},{16,24},{20,28},{0,8},{9,17},{13,21},{17,25},{21,29... | collective-permute-start | bytes 393224 | tf_op jit(solution)/shard_map/ppermute | solution.py:548
  55.8 4.7 %collective-permute-start.10 = (f32[32,1024]{1,0:T(8,128)S(1)}, f32[32,1024]{1,0:T(8,128)S(1)}, u32[]{:S(2)}, u32[]{:S(2)}) collective-permute-start(f32[32,1024]{1,0:T(8,128)S(1)} %get-tuple-element.67), channel_id=1, source_target_pairs={{8,20},{12,24},{16,28},{20,12},{0,8},{9,21},{13,25},{17,29},{21,13... | collective-permute-start | bytes 393224 | tf_op jit(solution)/shard_map/ppermute | solution.py:548
  60.5 1.9 %collective-permute-start.11 = (f32[32,1024]{1,0:T(8,128)S(1)}, f32[32,1024]{1,0:T(8,128)S(1)}, u32[]{:S(2)}, u32[]{:S(2)}) collective-permute-start(f32[32,1024]{1,0:T(8,128)S(1)} %get-tuple-element.68), channel_id=1, source_target_pairs={{8,24},{12,28},{16,12},{20,16},{0,8},{9,25},{13,29},{17,13},{21,17... | collective-permute-start | bytes 393224 | tf_op jit(solution)/shard_map/ppermute | solution.py:548
  63.1 8.5 %adjoint.1 = (f32[32,4096]{1,0:T(8,128)}, f32[32,384]{1,0:T(8,128)S(1)}) custom-call(f32[32,1024]{1,0:T(8,128)S(1)} %get-tuple-element.64.local_ref._, f32[32,4096]{1,0:T(8,128)S(1)} %bitcast.7, f32[32,4096]{1,0:T(8,128)S(1)} %collective-permute-done.13.lam_after_ref, f32[32,384]{1,0:T(8,128)S(1)} %copy-done.1, ...), custom_call_target="tpu_custom_call" | custom-call | flops 1000000000 | bytes 2097152 | tf_op jit(solution)/shard_map/adjoint/pallas_call | solution.py:551
  71.7 1.8 %collective-permute-start.15 = (f32[32,384]{1,0:T(8,128)S(1)}, f32[32,384]{1,0:T(8,128)S(1)}, u32[]{:S(2)}, u32[]{:S(2)}) collective-permute-start(f32[32,384]{1,0:T(8,128)S(1)} %get-tuple-element.75.refs_0_), channel_id=1, source_target_pairs={{0,2},{1,3},{2,0},{3,1},{4,6},{5,7},{6,4},{7,5},{8,10},{9,11},{10,... | collective-permute-start | bytes 147464 | tf_op jit(solution)/shard_map/ppermute | solution.py:482
  73.6 0.9 %collect.1 = f32[32,4096]{1,0:T(8,128)} custom-call(f32[32,4096]{1,0:T(8,128)S(1)} %get-tuple-element.48.point_ref, f32[32,1024]{1,0:T(8,128)S(1)} %get-tuple-element.64.local_ref._, f32[32,1024]{1,0:T(8,128)S(1)} %collective-permute-done.8.rest_0_, f32[32,1024]{1,0:T(8,128)S(1)} %collective-permute-done.9.rest_1_, ...), custom_call_target="tpu_custom_call" | custom-call | flops 50000000 | bytes 2097152 | tf_op jit(solution)/shard_map/collect/pallas_call | solution.py:556
  74.5 1.0 %collective-permute-done.16.refs_3_ = f32[32,384]{1,0:T(8,128)S(1)} collective-permute-done((f32[32,384]{1,0:T(8,128)S(1)}, f32[32,384]{1,0:T(8,128)S(1)}, u32[]{:S(2)}, u32[]{:S(2)}) %collective-permute-start.16) | collective-permute-done | bytes 49184 | tf_op jit(solution)/shard_map/ppermute | solution.py:482
  75.5 0.9 %collective-permute-done.15.refs_2_ = f32[32,384]{1,0:T(8,128)S(1)} collective-permute-done((f32[32,384]{1,0:T(8,128)S(1)}, f32[32,384]{1,0:T(8,128)S(1)}, u32[]{:S(2)}, u32[]{:S(2)}) %collective-permute-start.15) | collective-permute-done | bytes 49184 | tf_op jit(solution)/shard_map/ppermute | solution.py:482
  76.4 0.8 sum.1
  (26 shorter events, 1.0 us)
Async XLA Ops:
  2.7 14.3 %collective-permute-start.1 = (f32[32,128]{1,0:T(8,128)}, f32[32,128]{1,0:T(8,128)S(1)}, u32[]{:S(2)}, u32[]{:S(2)}) collective-permute-start(f32[32,128]{1,0:T(8,128)} %get-tuple-element.43), channel_id=1, source_target_pairs={{8,0},{9,1},{10,2},{11,3}} | collective-permute-start | bytes 49160 | tf_op jit(solution)/shard_map/ppermute | solution.py:508
  4.0 13.0 %collective-permute-start = (f32[32,384]{1,0:T(8,128)}, f32[32,384]{1,0:T(8,128)S(1)}, u32[]{:S(2)}, u32[]{:S(2)}) collective-permute-start(f32[32,384]{1,0:T(8,128)} %get-tuple-element.42.p_ref), channel_id=1, source_target_pairs={{4,0},{8,4},{12,8},{16,12},{20,16},{24,20},{28,24},{5,1},{9,5},{13... | collective-permute-start | bytes 147464 | tf_op jit(solution)/shard_map/ppermute | solution.py:476
  5.3 29.9 %copy-start = (f32[1,1,32,4096]{3,2,1,0:T(8,128)S(1)}, f32[1,1,32,4096]{3,2,1,0:T(8,128)}, u32[]{:S(2)}) copy-start(f32[1,1,32,4096]{3,2,1,0:T(8,128)} %param.7) | copy-start | bytes 1572868
  5.4 29.9 %collective-permute-start.2 = (f32[32,4480]{1,0:T(8,128)}, f32[32,4480]{1,0:T(8,128)S(1)}, u32[]{:S(2)}, u32[]{:S(2)}) collective-permute-start(f32[32,4480]{1,0:T(8,128)} %get-tuple-element.41.both_ref), channel_id=1, source_target_pairs={{0,4},{4,8},{8,12},{12,16},{16,20},{20,24},{24,28},{1,5},{5,9},{9,... | collective-permute-start | bytes 1720328 | tf_op jit(solution)/shard_map/ppermute | solution.py:476
  10.4 1.1 %copy-start.2 = (f32[32,4480]{1,0:T(8,128)S(1)}, f32[32,4480]{1,0:T(8,128)}, u32[]{:S(2)}) copy-start(f32[32,4480]{1,0:T(8,128)} %get-tuple-element.41.both_ref) | copy-start | bytes 1720324
  11.4 23.8 %copy-start.3 = (f32[32,4480]{1,0:T(8,128)S(1)}, f32[32,4480]{1,0:T(8,128)}, u32[]{:S(2)}) copy-start(f32[32,4480]{1,0:T(8,128)} %get-tuple-element.41.both_ref) | copy-start | bytes 1720324
  17.0 25.2 %copy-start.1 = (f32[32,384]{1,0:T(8,128)S(1)}, f32[32,384]{1,0:T(8,128)}, u32[]{:S(2)}) copy-start(f32[32,384]{1,0:T(8,128)} %get-tuple-element.42.p_ref) | copy-start | bytes 147460
  19.2 13.4 %collective-permute-start.3 = (f32[32,1664]{1,0:T(8,128)S(1)}, f32[32,1664]{1,0:T(8,128)S(1)}, u32[]{:S(2)}, u32[]{:S(2)}) collective-permute-start(f32[32,1664]{1,0:T(8,128)S(1)} %get-tuple-element.50), channel_id=1, source_target_pairs={{0,8},{4,12},{8,16},{12,20},{1,9},{5,13},{9,17},{13,21},{2,10},{6,... | collective-permute-start | bytes 638984 | tf_op jit(solution)/shard_map/ppermute | solution.py:525
  20.8 20.2 %collective-permute-start.4 = (f32[32,1664]{1,0:T(8,128)S(1)}, f32[32,1664]{1,0:T(8,128)S(1)}, u32[]{:S(2)}, u32[]{:S(2)}) collective-permute-start(f32[32,1664]{1,0:T(8,128)S(1)} %get-tuple-element.51), channel_id=1, source_target_pairs={{4,8},{8,12},{12,16},{16,20},{5,9},{9,13},{13,17},{17,21},{6,10},{... | collective-permute-start | bytes 638984 | tf_op jit(solution)/shard_map/ppermute | solution.py:525
  21.4 19.5 %collective-permute-start.5 = (f32[32,1664]{1,0:T(8,128)S(1)}, f32[32,1664]{1,0:T(8,128)S(1)}, u32[]{:S(2)}, u32[]{:S(2)}) collective-permute-start(f32[32,1664]{1,0:T(8,128)S(1)} %get-tuple-element.52), channel_id=1, source_target_pairs={{12,8},{16,12},{20,16},{0,20},{13,9},{17,13},{21,17},{1,21},{14,10... | collective-permute-start | bytes 638984 | tf_op jit(solution)/shard_map/ppermute | solution.py:525
  27.4 13.6 %collective-permute-start.6 = (f32[32,1664]{1,0:T(8,128)S(1)}, f32[32,1664]{1,0:T(8,128)S(1)}, u32[]{:S(2)}, u32[]{:S(2)}) collective-permute-start(f32[32,1664]{1,0:T(8,128)S(1)} %get-tuple-element.53), channel_id=1, source_target_pairs={{16,8},{20,12},{0,16},{4,20},{17,9},{21,13},{1,17},{5,21},{18,10},... | collective-permute-start | bytes 638984 | tf_op jit(solution)/shard_map/ppermute | solution.py:525
  32.6 8.4 %collective-permute-start.7 = (f32[32,1664]{1,0:T(8,128)S(1)}, f32[32,1664]{1,0:T(8,128)S(1)}, u32[]{:S(2)}, u32[]{:S(2)}) collective-permute-start(f32[32,1664]{1,0:T(8,128)S(1)} %get-tuple-element.55), channel_id=1, source_target_pairs={{20,8},{0,12},{4,16},{8,20},{21,9},{1,13},{5,17},{9,21},{22,10},{2... | collective-permute-start | bytes 638984 | tf_op jit(solution)/shard_map/ppermute | solution.py:525
  41.0 21.4 %collective-permute-start.13 = (f32[32,4096]{1,0:T(8,128)S(1)}, f32[32,4096]{1,0:T(8,128)S(1)}, u32[]{:S(2)}, u32[]{:S(2)}) collective-permute-start(f32[32,4096]{1,0:T(8,128)S(1)} %get-tuple-element.56._), channel_id=1, source_target_pairs={{4,0},{8,4},{12,8},{16,12},{20,16},{24,20},{28,24},{5,1},{9,5},{13... | collective-permute-start | bytes 1572872 | tf_op jit(solution)/shard_map/ppermute | solution.py:476
  42.4 29.2 %collective-permute-start.8 = (f32[32,1024]{1,0:T(8,128)S(1)}, f32[32,1024]{1,0:T(8,128)S(1)}, u32[]{:S(2)}, u32[]{:S(2)}) collective-permute-start(f32[32,1024]{1,0:T(8,128)S(1)} %get-tuple-element.65), channel_id=1, source_target_pairs={{8,12},{12,16},{16,20},{20,24},{0,8},{9,13},{13,17},{17,21},{21,25... | collective-permute-start | bytes 393224 | tf_op jit(solution)/shard_map/ppermute | solution.py:548
  52.6 19.0 %collective-permute-start.9 = (f32[32,1024]{1,0:T(8,128)S(1)}, f32[32,1024]{1,0:T(8,128)S(1)}, u32[]{:S(2)}, u32[]{:S(2)}) collective-permute-start(f32[32,1024]{1,0:T(8,128)S(1)} %get-tuple-element.66), channel_id=1, source_target_pairs={{8,16},{12,20},{16,24},{20,28},{0,8},{9,17},{13,21},{17,25},{21,29... | collective-permute-start | bytes 393224 | tf_op jit(solution)/shard_map/ppermute | solution.py:548
  55.8 15.8 %collective-permute-start.10 = (f32[32,1024]{1,0:T(8,128)S(1)}, f32[32,1024]{1,0:T(8,128)S(1)}, u32[]{:S(2)}, u32[]{:S(2)}) collective-permute-start(f32[32,1024]{1,0:T(8,128)S(1)} %get-tuple-element.67), channel_id=1, source_target_pairs={{8,20},{12,24},{16,28},{20,12},{0,8},{9,21},{13,25},{17,29},{21,13... | collective-permute-start | bytes 393224 | tf_op jit(solution)/shard_map/ppermute | solution.py:548
  60.5 11.1 %collective-permute-start.11 = (f32[32,1024]{1,0:T(8,128)S(1)}, f32[32,1024]{1,0:T(8,128)S(1)}, u32[]{:S(2)}, u32[]{:S(2)}) collective-permute-start(f32[32,1024]{1,0:T(8,128)S(1)} %get-tuple-element.68), channel_id=1, source_target_pairs={{8,24},{12,28},{16,12},{20,16},{0,8},{9,25},{13,29},{17,13},{21,17... | collective-permute-start | bytes 393224 | tf_op jit(solution)/shard_map/ppermute | solution.py:548
  62.4 9.2 %collective-permute-start.12 = (f32[32,1024]{1,0:T(8,128)S(1)}, f32[32,1024]{1,0:T(8,128)S(1)}, u32[]{:S(2)}, u32[]{:S(2)}) collective-permute-start(f32[32,1024]{1,0:T(8,128)S(1)} %get-tuple-element.64.local_ref._), channel_id=1, source_target_pairs={{8,28},{9,29},{10,30},{11,31}} | collective-permute-start | bytes 393224 | tf_op jit(solution)/shard_map/ppermute | solution.py:548
  71.6 3.8 %collective-permute-start.16 = (f32[32,384]{1,0:T(8,128)S(1)}, f32[32,384]{1,0:T(8,128)S(1)}, u32[]{:S(2)}, u32[]{:S(2)}) collective-permute-start(f32[32,384]{1,0:T(8,128)S(1)} %get-tuple-element.75.refs_0_), channel_id=1, source_target_pairs={{0,3},{1,2},{2,1},{3,0},{4,7},{5,6},{6,5},{7,4},{8,11},{9,10},{10,... | collective-permute-start | bytes 147464 | tf_op jit(solution)/shard_map/ppermute | solution.py:482
  71.7 4.7 %collective-permute-start.15 = (f32[32,384]{1,0:T(8,128)S(1)}, f32[32,384]{1,0:T(8,128)S(1)}, u32[]{:S(2)}, u32[]{:S(2)}) collective-permute-start(f32[32,384]{1,0:T(8,128)S(1)} %get-tuple-element.75.refs_0_), channel_id=1, source_target_pairs={{0,2},{1,3},{2,0},{3,1},{4,6},{5,7},{6,4},{7,5},{8,10},{9,11},{10,... | collective-permute-start | bytes 147464 | tf_op jit(solution)/shard_map/ppermute | solution.py:482
  73.5 2.9 %collective-permute-start.14 = (f32[32,384]{1,0:T(8,128)S(1)}, f32[32,384]{1,0:T(8,128)S(1)}, u32[]{:S(2)}, u32[]{:S(2)}) collective-permute-start(f32[32,384]{1,0:T(8,128)S(1)} %get-tuple-element.75.refs_0_), channel_id=1, source_target_pairs={{0,1},{1,0},{2,3},{3,2},{4,5},{5,4},{6,7},{7,6},{8,9},{9,8},{10,11... | collective-permute-start | bytes 147464 | tf_op jit(solution)/shard_map/ppermute | solution.py:482
where the time goes:
time: 76 us; the launch traced here: 77.1 us
  starting transfers between devices  47.5 us (62%)
  Pallas kernels  25.7 us (34%)
  waiting for transfers between devices  1.95 us (3%)
  local copies, waits for them, and re-layouts  1.09 us (1%)
  between operations  0.93 us (1%)
    ppermute x5, starting transfers between devices, body(): lax.ppermute(block, 'depth', plan.out_pairs(k))  20.6 us
    ppermute x5, starting transfers between devices, body(): arrived[shift] = lax.ppermute(msg, 'depth', plan.in_pairs(shift))  16 us
    pallas_call x1, Pallas kernels, body(): call(adjoint_kernel, [state, shape(rows, wide)], [ANY] + [VMEM] * 7, [buf...  8.5 us
    ppermute x3, starting transfers between devices, shifted(): lax.ppermute(value, 'depth', [(s, s + steps) for s in range(first, end)])  7.59 us
    pallas_call x1, Pallas kernels, body(): call(point_kernel, [state] * 2 + [saved] * 4, [ANY] + [VMEM] * 3, [buffer...  5.64 us
    pallas_call x1, Pallas kernels, body(): call(push_kernel, state, [VMEM], [buffer, *factors], 40, 'push')(both)  5.57 us
    pallas_call x1, Pallas kernels, body(): call(functools.partial(tau_kernel, plan), [state] + [window] * plan.items...  2.12 us
    pallas_call x1, Pallas kernels, body(): call(pack_kernel, [shape(rows, wide), shape(rows, LANES), shape(rows, wid...  2.1 us
  transfers between devices with their start and end apart: 17, of which 2 were waited for; matrix products, arithmetic and copies ran while one was open for 0% of the time, Pallas kernels for 30%

commit v1 on v0

--- a/solution.py
+++ b/solution.py
@@ -44,30 +44,66 @@
     return col > 0, col < IMG - 1, lane < IMG
 
 
-def neighbours(left, mid, right, masks):
-    not_first, not_last, upper = masks
-    pieces = [left] + [mid[:, k : k + LANES] for k in range(0, mid.shape[1], LANES)] + [right]
-    swapped = [pltpu.roll(piece, IMG, 1) for piece in pieces]
+def swap(piece):
+    return pltpu.roll(piece, IMG, 1)
+
+
+def pieces_of(x):
+    return [x[:, k : k + LANES] for k in range(0, x.shape[1], LANES)]
+
+
+def to_pairs(x):
+    pieces = pieces_of(x)
+    half = len(pieces) // 2
+    lower = lane_masks(x.shape[0])[2]
+    out = []
+    for k in range(half):
+        out.append(jnp.where(lower, pieces[k], swap(pieces[k + half])))
+        out.append(jnp.where(lower, swap(pieces[k]), pieces[k + half]))
+    return jnp.concatenate(out, axis=1)
+
+
+def from_pairs(x):
+    pieces = pieces_of(x)
+    half = len(pieces) // 2
+    lower = lane_masks(x.shape[0])[2]
+    first = [jnp.where(lower, pieces[2 * k], swap(pieces[2 * k + 1])) for k in range(half)]
+    second = [jnp.where(lower, swap(pieces[2 * k]), pieces[2 * k + 1]) for k in range(half)]
+    return jnp.concatenate(first + second, axis=1)
+
+
+def neighbours(left, mid, right, masks, paired):
+    not_first, not_last, lower = masks
+    pieces = [left] + pieces_of(mid) + [right]
+    swapped = None if paired else [swap(piece) for piece in pieces]
     sums = []
     for k in range(1, len(pieces) - 1):
         piece = pieces[k]
         beside = jnp.where(not_first, pltpu.roll(piece, 1, 1), 0.0)
         beside += jnp.where(not_last, pltpu.roll(piece, LANES - 1, 1), 0.0)
-        beside += swapped[k] + jnp.where(upper, swapped[k - 1], swapped[k + 1])
+        if paired:
+            beside += pieces[k - 1] + pieces[k + 1]
+        else:
+            beside += swapped[k] + jnp.where(lower, swapped[k - 1], swapped[k + 1])
         sums.append(beside)
     return jnp.concatenate(sums, axis=1)
 
 
-def sweep(buf, width, step):
+def sweep(buf, width, step, paired):
     rows = buf.shape[0]
     masks = lane_masks(rows)
-    before = buf[:, 0:LANES]
+    if paired:
+        lower = masks[2]
+        before = jnp.where(lower, 0.0, swap(buf[:, width : width + LANES]))
+        buf[:, width + LANES :] = jnp.where(lower, swap(buf[:, LANES : 2 * LANES]), 0.0)
+    else:
+        before = buf[:, 0:LANES]
     for start in range(0, width, CHUNK):
         size = min(CHUNK, width - start)
         at = LANES + start
         mid = buf[:, at : at + size]
         after = buf[:, at + size : at + size + LANES]
-        around = neighbours(before, mid, after, masks)
+        around = neighbours(before, mid, after, masks, paired)
         before = mid[:, size - LANES :]
         buf[:, at : at + size] = step(start, size, mid, around)
 
@@ -146,7 +182,7 @@
     copies[-1].wait()
 
 
-def forward_layer(buf, width, wl, wt, bias, spread, t_out=None, u_out=None):
+def forward_layer(buf, width, wl, wt, bias, spread, t_out=None, u_out=None, paired=True):
     keep = 1.0 - 4.0 * spread
 
     def step(start, size, mid, around):
@@ -158,7 +194,7 @@
             u_out(start, size, hi, lo)
         return mid * keep + around * spread - mm(wt, stack3(t_hi, t_lo))
 
-    sweep(buf, width, step)
+    sweep(buf, width, step, paired)
 
 
 def run_forward(buf, width, p_ref, wl_ref, wt_ref, spread, count, t_refs=None, u_refs=None):
@@ -203,7 +239,7 @@
                 sums.append(sum(q[:, k : k + LANES] for k in range(0, size, LANES)))
             return mid * keep + around * spread - mm(wt, stack3(q_hi, q_lo))
 
-        sweep(buf, width, step)
+        sweep(buf, width, step, True)
         if grads is not None:
             g_ref, factor, lam_ref, q_ref = grads
 
@@ -262,7 +298,7 @@
     width = out_ref.shape[1]
     p_ref = both_ref.at[:, width:]
     spread, _ = prepare(p_ref, wl, wt)
-    fill(buf, both_ref[:, 0:width])
+    fill(buf, to_pairs(both_ref[:, 0:width]))
     run_forward(buf, width, p_ref, wl, wt, spread, length_of(p_ref, lax.axis_index("depth")))
     out_ref[...] = inner(buf)
 
@@ -275,7 +311,7 @@
     spread, factor = prepare(p_ref, wl, wt)
     fill(buf, point_ref[...])
     run_forward(buf, width, p_ref, wl, wt, spread, count)
-    second_ref[...] = inner(buf)
+    whole[...] = inner(buf)
 
     def coarse(matrix, bias, length):
         scale = length.astype(F32)
@@ -287,12 +323,13 @@
     def _():
         buf[:, LANES : LANES + width] = point_ref[...]
         coarse(matrix_of(p_ref, 0), bias_of(p_ref, 0), count)
-        whole[...] = second_ref[...] - inner(buf)
+        whole[...] = from_pairs(whole[...] - inner(buf))
 
     @pl.when(own == 0)
     def _():
+        second_ref[...] = from_pairs(whole[...])
         coarse(p2_ref[:, 0:rows], p2_ref[:, rows : rows + 1], length_of(p_ref, 2))
-        whole[...] = inner(buf)
+        whole[...] = from_pairs(inner(buf))
 
     size = plan.rows * IMG
     bias = bias_of(p_ref, 0)
@@ -313,14 +350,17 @@
         p_before_ref = before_ref.at[:, width:]
         count = length_of(p_before_ref, jnp.maximum(own - 1, 0))
         spread, _ = prepare(p_before_ref, wl, wt)
-        fill(buf, before_ref[:, 0:width])
+        fill(buf, to_pairs(before_ref[:, 0:width]))
         run_forward(buf, width, p_before_ref, wl, wt, spread, count)
-        point_ref[...] = inner(buf)
+
+    @pl.when(own == 1)
+    def _():
+        point_ref[...] = from_pairs(inner(buf))
 
     @pl.when(own == 0)
     def _():
         point_ref[...] = both_ref[:, 0:width]
-        fill(buf, both_ref[:, 0:width])
+        fill(buf, to_pairs(both_ref[:, 0:width]))
 
     p_ref = both_ref.at[:, width:]
     count = length_of(p_ref, own)
@@ -329,7 +369,7 @@
 
     @pl.when(own > 0)
     def _():
-        fill(buf, adj_ref[...])
+        fill(buf, to_pairs(adj_ref[...]))
         run_backward(buf, width, wl, wt, spread, count, (t_hi, t_lo))
         lam_ref[...] = inner(buf)
 
@@ -348,14 +388,14 @@
 
     @pl.when(own == last)
     def _():
-        fill(buf, adj_ref[...])
+        fill(buf, to_pairs(adj_ref[...]))
 
     spread, factor = prepare(p_ref, wl, wt)
     run_backward(
         buf, width, wl, wt, spread, length_of(p_ref, own), (t_hi, t_lo), (u_hi, u_lo),
         (g_all, factor, lam_ref, q_ref),
     )
-    adj_out_ref[...] = inner(buf)
+    adj_out_ref[...] = from_pairs(inner(buf))
     most = g_all.shape[0]
     g_ref[:, most * rows :] = jnp.zeros((rows, LANES), F32)
     for slot in range(most):
@@ -410,7 +450,7 @@
         def _(item):
             forward_layer(
                 buf, size, wl[item], wt[item], held[item, :, size + rows : size + rows + 1],
-                length_of(p_ref, item + 1).astype(F32) * spread,
+                length_of(p_ref, item + 1).astype(F32) * spread, paired=False,
             )
             buf[:, LANES : LANES + size] = inner(buf) + held[item, :, 0:size]
             keep(item - 1)
@@ -528,7 +568,6 @@
     point, lam, *kept = call(
         point_kernel, [state] * 2 + [saved] * 4, [ANY] + [VMEM] * 3, [buffer, *factors], 6, "point"
     )(msgs[plan.first], both, before, adjoint)
-    lam, msgs = lax.optimization_barrier((lam, msgs))
     lam_after = shifted(lam, -1)
 
     piece = shape(rows, plan.block * IMG)
@@ -543,7 +582,7 @@
             pltpu.VMEM((plan.items, rows, 3 * rows), BF16),
             pltpu.SemaphoreType.DMA((plan.items,)),
         ],
-        1, "chain",
+        40, "chain",
     )(lam, second, packed, *msgs)
     received = [lax.ppermute(block, "depth", plan.out_pairs(k)) for k, block in enumerate(blocks)]
 

time: 76 us -> 75.1 us (0.988)
  the two profiles are of different devices: /device:TPU:0 before, /device:TPU:19 now
where the time goes in v1:
time: 75.1 us; the launch traced here: 73.9 us
  starting transfers between devices  36.8 us (49%)
  Pallas kernels  33.1 us (44%)
  waiting for transfers between devices  2.05 us (3%)
  local copies, waits for them, and re-layouts  1.08 us (1%)
  between operations  0.93 us (1%)
    ppermute x5, starting transfers between devices, body(): arrived[shift] = lax.ppermute(msg, 'depth', plan.in_pairs(shift))  12.5 us
    pallas_call x1, Pallas kernels, body(): call(point_kernel, [state] * 2 + [saved] * 4, [ANY] + [VMEM] * 3, [buffer...  10.2 us
    ppermute x5, starting transfers between devices, body(): lax.ppermute(block, 'depth', plan.out_pairs(k))  9.17 us
    pallas_call x1, Pallas kernels, body(): call(adjoint_kernel, [state, shape(rows, wide)], [ANY] + [VMEM] * 7, [buf...  8.67 us
    ppermute x3, starting transfers between devices, shifted(): lax.ppermute(value, 'depth', [(s, s + steps) for s in range(first, end)])  8.23 us
    ppermute x3, starting transfers between devices, others(): lax.ppermute(value, 'batch', [(s, s ^ step if xor else (s + step) % count...  6.2 us
    pallas_call x1, Pallas kernels, body(): call(push_kernel, state, [VMEM], [buffer, *factors], 40, 'push')(both)  4.98 us
    pallas_call x1, Pallas kernels, body(): call(functools.partial(chain_kernel, plan), [piece] * plan.results, [ANY,...  3.56 us
  transfers between devices with their start and end apart: 17, of which 2 were waited for; matrix products, arithmetic and copies ran while one was open for 0% of the time, Pallas kernels for 41%

profile of v1, /device:TPU:19, one launch (start us, length us, event | category | flops | bytes accessed | tf_op | source)
XLA Modules:
  0.0 73.9 jit_solution(5839685823527575444)
XLA Ops:
  0.6 2.1 %pack.1 = (f32[32,384]{1,0:T(8,128)}, f32[32,128]{1,0:T(8,128)}, f32[32,4480]{1,0:T(8,128)}) custom-call(f32[8,32,32]{2,1,0:T(8,128)} %w_any.1, f32[8,32]{1,0:T(8,128)} %b_any.1, f32[1,32]{1,0:T(1,128)} %bitcast.10, s32[1,8]{1,0:T(1,128)} %bitcast.11, f32[32,4096]{1,0:T(8,128)} %bitcast.9), custom_call_target="tpu_custom_call" | custom-call | flops 100000000 | bytes 2097152 | tf_op jit(solution)/shard_map/pack/pallas_call | solution.py:539
  3.4 2.2 %collective-permute-start = (f32[32,384]{1,0:T(8,128)}, f32[32,384]{1,0:T(8,128)S(1)}, u32[]{:S(2)}, u32[]{:S(2)}) collective-permute-start(f32[32,384]{1,0:T(8,128)} %get-tuple-element.35.p_ref), channel_id=1, source_target_pairs={{4,0},{8,4},{12,8},{16,12},{20,16},{24,20},{28,24},{5,1},{9,5},{13... | collective-permute-start | bytes 147464 | tf_op jit(solution)/shard_map/ppermute | solution.py:516
  5.6 4.1 %collective-permute-start.2 = (f32[32,4480]{1,0:T(8,128)}, f32[32,4480]{1,0:T(8,128)S(1)}, u32[]{:S(2)}, u32[]{:S(2)}) collective-permute-start(f32[32,4480]{1,0:T(8,128)} %get-tuple-element.34.both_ref), channel_id=1, source_target_pairs={{0,4},{4,8},{8,12},{12,16},{16,20},{20,24},{24,28},{1,5},{5,9},{9,... | collective-permute-start | bytes 1720328 | tf_op jit(solution)/shard_map/ppermute | solution.py:516
  9.8 1.1 %copy-done.2 = f32[32,4480]{1,0:T(8,128)S(1)} copy-done((f32[32,4480]{1,0:T(8,128)S(1)}, f32[32,4480]{1,0:T(8,128)}, u32[]{:S(2)}) %copy-start.2) | copy-done | bytes 573464
  10.8 5.0 %push.1.point_ref = f32[32,4096]{1,0:T(8,128)S(1)} custom-call(f32[32,4480]{1,0:T(8,128)S(1)} %copy-done.2), custom_call_target="tpu_custom_call" | custom-call | flops 4000000000 | bytes 2097152 | tf_op jit(solution)/shard_map/push/pallas_call | solution.py:550
  15.8 1.9 %tau.1 = (f32[32,4096]{1,0:T(8,128)S(1)}, f32[32,1664]{1,0:T(8,128)S(1)}, f32[32,1664]{1,0:T(8,128)S(1)}, f32[32,1664]{1,0:T(8,128)S(1)}, f32[32,1664]{1,0:T(8,1...) custom-call(f32[32,4096]{1,0:T(8,128)S(1)} %push.1.point_ref, f32[32,384]{1,0:T(8,128)S(1)} %collective-permute-done.p_ref, ...), custom_call_target="tpu_custom_call" | custom-call | flops 300000000 | bytes 2097152 | tf_op jit(solution)/shard_map/tau/pallas_call | solution.py:555
  17.8 1.3 %collective-permute-start.3 = (f32[32,1664]{1,0:T(8,128)S(1)}, f32[32,1664]{1,0:T(8,128)S(1)}, u32[]{:S(2)}, u32[]{:S(2)}) collective-permute-start(f32[32,1664]{1,0:T(8,128)S(1)} %get-tuple-element.44), channel_id=1, source_target_pairs={{0,8},{4,12},{8,16},{12,20},{1,9},{5,13},{9,17},{13,21},{2,10},{6,... | collective-permute-start | bytes 638984 | tf_op jit(solution)/shard_map/ppermute | solution.py:565
  19.1 1.3 %collective-permute-start.4 = (f32[32,1664]{1,0:T(8,128)S(1)}, f32[32,1664]{1,0:T(8,128)S(1)}, u32[]{:S(2)}, u32[]{:S(2)}) collective-permute-start(f32[32,1664]{1,0:T(8,128)S(1)} %get-tuple-element.45), channel_id=1, source_target_pairs={{4,8},{8,12},{12,16},{16,20},{5,9},{9,13},{13,17},{17,21},{6,10},{... | collective-permute-start | bytes 638984 | tf_op jit(solution)/shard_map/ppermute | solution.py:565
  20.4 4.0 %collective-permute-start.5 = (f32[32,1664]{1,0:T(8,128)S(1)}, f32[32,1664]{1,0:T(8,128)S(1)}, u32[]{:S(2)}, u32[]{:S(2)}) collective-permute-start(f32[32,1664]{1,0:T(8,128)S(1)} %get-tuple-element.46), channel_id=1, source_target_pairs={{12,8},{16,12},{20,16},{0,20},{13,9},{17,13},{21,17},{1,21},{14,10... | collective-permute-start | bytes 638984 | tf_op jit(solution)/shard_map/ppermute | solution.py:565
  24.4 4.0 %collective-permute-start.6 = (f32[32,1664]{1,0:T(8,128)S(1)}, f32[32,1664]{1,0:T(8,128)S(1)}, u32[]{:S(2)}, u32[]{:S(2)}) collective-permute-start(f32[32,1664]{1,0:T(8,128)S(1)} %get-tuple-element.47), channel_id=1, source_target_pairs={{16,8},{20,12},{0,16},{4,20},{17,9},{21,13},{1,17},{5,21},{18,10},... | collective-permute-start | bytes 638984 | tf_op jit(solution)/shard_map/ppermute | solution.py:565
  28.4 1.9 %collective-permute-start.7 = (f32[32,1664]{1,0:T(8,128)S(1)}, f32[32,1664]{1,0:T(8,128)S(1)}, u32[]{:S(2)}, u32[]{:S(2)}) collective-permute-start(f32[32,1664]{1,0:T(8,128)S(1)} %get-tuple-element.49), channel_id=1, source_target_pairs={{20,8},{0,12},{4,16},{8,20},{21,9},{1,13},{5,17},{9,21},{22,10},{2... | collective-permute-start | bytes 638984 | tf_op jit(solution)/shard_map/ppermute | solution.py:565
  30.4 10.2 %point.1 = (f32[32,4096]{1,0:T(8,128)S(1)}, f32[32,4096]{1,0:T(8,128)S(1)}, bf16[8,32,4096]{2,1,0:T(8,128)(2,1)S(1)}, bf16[8,32,4096]{2,1,0:T(8,128)(2,1)S(1)}, ...) custom-call(f32[32,1664]{1,0:T(8,128)S(1)} %get-tuple-element.40._.rest_2_, f32[32,4480]{1,0:T(8,128)S(1)} %copy-done.3, ...), custom_call_target="tpu_custom_call" | custom-call | flops 600000000 | bytes 2097152 | tf_op jit(solution)/shard_map/point/pallas_call | solution.py:568
  40.6 1.9 %collective-permute-start.13 = (f32[32,4096]{1,0:T(8,128)S(1)}, f32[32,4096]{1,0:T(8,128)S(1)}, u32[]{:S(2)}, u32[]{:S(2)}) collective-permute-start(f32[32,4096]{1,0:T(8,128)S(1)} %get-tuple-element.42._), channel_id=1, source_target_pairs={{4,0},{8,4},{12,8},{16,12},{20,16},{24,20},{28,24},{5,1},{9,5},{13... | collective-permute-start | bytes 1572872 | tf_op jit(solution)/shard_map/ppermute | solution.py:516
  42.6 3.6 %chain.1 = (f32[32,1024]{1,0:T(8,128)S(1)}, f32[32,1024]{1,0:T(8,128)S(1)}, f32[32,1024]{1,0:T(8,128)S(1)}, f32[32,1024]{1,0:T(8,128)S(1)}, f32[32,1024]{1,0:T(8,128)S(1)}) custom-call(f32[32,4096]{1,0:T(8,128)S(1)} %get-tuple-element.42._, f32[32,4096]{1,0:T(8,128)S(1)} %get-tuple-element.43.second_ref, f32[32,384]{1,0:T(8,128)S(1)} %copy-done.1, ...), custom_call_target="tpu_custom_call" | custom-call | flops 4000000000 | bytes 2097152 | tf_op jit(solution)/shard_map/chain/pallas_call | solution.py:574
  46.1 1.9 %collective-permute-start.8 = (f32[32,1024]{1,0:T(8,128)S(1)}, f32[32,1024]{1,0:T(8,128)S(1)}, u32[]{:S(2)}, u32[]{:S(2)}) collective-permute-start(f32[32,1024]{1,0:T(8,128)S(1)} %get-tuple-element.51), channel_id=1, source_target_pairs={{8,12},{12,16},{16,20},{20,24},{0,8},{9,13},{13,17},{17,21},{21,25... | collective-permute-start | bytes 393224 | tf_op jit(solution)/shard_map/ppermute | solution.py:587
  48.1 1.9 %collective-permute-start.9 = (f32[32,1024]{1,0:T(8,128)S(1)}, f32[32,1024]{1,0:T(8,128)S(1)}, u32[]{:S(2)}, u32[]{:S(2)}) collective-permute-start(f32[32,1024]{1,0:T(8,128)S(1)} %get-tuple-element.52), channel_id=1, source_target_pairs={{8,16},{12,20},{16,24},{20,28},{0,8},{9,17},{13,21},{17,25},{21,29... | collective-permute-start | bytes 393224 | tf_op jit(solution)/shard_map/ppermute | solution.py:587
  50.0 3.4 %collective-permute-start.10 = (f32[32,1024]{1,0:T(8,128)S(1)}, f32[32,1024]{1,0:T(8,128)S(1)}, u32[]{:S(2)}, u32[]{:S(2)}) collective-permute-start(f32[32,1024]{1,0:T(8,128)S(1)} %get-tuple-element.53), channel_id=1, source_target_pairs={{8,20},{12,24},{16,28},{20,12},{0,8},{9,21},{13,25},{17,29},{21,13... | collective-permute-start | bytes 393224 | tf_op jit(solution)/shard_map/ppermute | solution.py:587
  53.4 1.3 %collective-permute-start.11 = (f32[32,1024]{1,0:T(8,128)S(1)}, f32[32,1024]{1,0:T(8,128)S(1)}, u32[]{:S(2)}, u32[]{:S(2)}) collective-permute-start(f32[32,1024]{1,0:T(8,128)S(1)} %get-tuple-element.54), channel_id=1, source_target_pairs={{8,24},{12,28},{16,12},{20,16},{0,8},{9,25},{13,29},{17,13},{21,17... | collective-permute-start | bytes 393224 | tf_op jit(solution)/shard_map/ppermute | solution.py:587
  55.4 8.7 %adjoint.1 = (f32[32,4096]{1,0:T(8,128)}, f32[32,384]{1,0:T(8,128)S(1)}) custom-call(f32[32,1024]{1,0:T(8,128)S(1)} %get-tuple-element.50.local_ref._, f32[32,4096]{1,0:T(8,128)S(1)} %bitcast.7, f32[32,4096]{1,0:T(8,128)S(1)} %collective-permute-done.13.lam_after_ref, f32[32,384]{1,0:T(8,128)S(1)} %copy-done.1, ...), custom_call_target="tpu_custom_call" | custom-call | flops 1000000000 | bytes 2097152 | tf_op jit(solution)/shard_map/adjoint/pallas_call | solution.py:590
  64.1 5.7 %collective-permute-start.16 = (f32[32,384]{1,0:T(8,128)S(1)}, f32[32,384]{1,0:T(8,128)S(1)}, u32[]{:S(2)}, u32[]{:S(2)}) collective-permute-start(f32[32,384]{1,0:T(8,128)S(1)} %get-tuple-element.61.refs_0_), channel_id=1, source_target_pairs={{0,3},{1,2},{2,1},{3,0},{4,7},{5,6},{6,5},{7,4},{8,11},{9,10},{10,... | collective-permute-start | bytes 147464 | tf_op jit(solution)/shard_map/ppermute | solution.py:522
  70.3 0.9 %collect.1 = f32[32,4096]{1,0:T(8,128)} custom-call(f32[32,4096]{1,0:T(8,128)S(1)} %get-tuple-element.41.point_ref, f32[32,1024]{1,0:T(8,128)S(1)} %get-tuple-element.50.local_ref._, f32[32,1024]{1,0:T(8,128)S(1)} %collective-permute-done.8.rest_0_, f32[32,1024]{1,0:T(8,128)S(1)} %collective-permute-done.9.rest_1_, ...), custom_call_target="tpu_custom_call" | custom-call | flops 50000000 | bytes 2097152 | tf_op jit(solution)/shard_map/collect/pallas_call | solution.py:595
  71.1 1.1 %collective-permute-done.16.refs_3_ = f32[32,384]{1,0:T(8,128)S(1)} collective-permute-done((f32[32,384]{1,0:T(8,128)S(1)}, f32[32,384]{1,0:T(8,128)S(1)}, u32[]{:S(2)}, u32[]{:S(2)}) %collective-permute-start.16) | collective-permute-done | bytes 49184 | tf_op jit(solution)/shard_map/ppermute | solution.py:522
  72.2 0.9 %collective-permute-done.15.refs_2_ = f32[32,384]{1,0:T(8,128)S(1)} collective-permute-done((f32[32,384]{1,0:T(8,128)S(1)}, f32[32,384]{1,0:T(8,128)S(1)}, u32[]{:S(2)}, u32[]{:S(2)}) %collective-permute-start.15) | collective-permute-done | bytes 49184 | tf_op jit(solution)/shard_map/ppermute | solution.py:522
  73.2 0.8 %sum.1 = (f32[8,32,32]{2,1,0:T(8,128)}, f32[8,32]{1,0:T(8,128)}) custom-call(f32[32,384]{1,0:T(8,128)S(1)} %get-tuple-element.61.refs_0_, f32[32,384]{1,0:T(8,128)S(1)} %collective-permute-done.14.refs_1_, f32[32,384]{1,0:T(8,128)S(1)} %collective-permute-done.15.refs_2_, f32[32,384]{1,0:T(8,128)S(1)} %collective-permute-done.16.refs_3_), custom_call_target="tpu_custom_call" | custom-call | flops 50000000 | bytes 2097152 | tf_op jit(solution)/shard_map/sum/pallas_call | solution.py:600
  (26 shorter events, 1.9 us)
Async XLA Ops:
  2.7 13.1 %collective-permute-start.1 = (f32[32,128]{1,0:T(8,128)}, f32[32,128]{1,0:T(8,128)S(1)}, u32[]{:S(2)}, u32[]{:S(2)}) collective-permute-start(f32[32,128]{1,0:T(8,128)} %get-tuple-element.36), channel_id=1, source_target_pairs={{8,0},{9,1},{10,2},{11,3}} | collective-permute-start | bytes 49160 | tf_op jit(solution)/shard_map/ppermute | solution.py:548
  3.4 12.4 %collective-permute-start = (f32[32,384]{1,0:T(8,128)}, f32[32,384]{1,0:T(8,128)S(1)}, u32[]{:S(2)}, u32[]{:S(2)}) collective-permute-start(f32[32,384]{1,0:T(8,128)} %get-tuple-element.35.p_ref), channel_id=1, source_target_pairs={{4,0},{8,4},{12,8},{16,12},{20,16},{24,20},{28,24},{5,1},{9,5},{13... | collective-permute-start | bytes 147464 | tf_op jit(solution)/shard_map/ppermute | solution.py:516
  5.6 24.8 %copy-start = (f32[1,1,32,4096]{3,2,1,0:T(8,128)S(1)}, f32[1,1,32,4096]{3,2,1,0:T(8,128)}, u32[]{:S(2)}) copy-start(f32[1,1,32,4096]{3,2,1,0:T(8,128)} %param.7) | copy-start | bytes 1572868
  5.6 24.7 %collective-permute-start.2 = (f32[32,4480]{1,0:T(8,128)}, f32[32,4480]{1,0:T(8,128)S(1)}, u32[]{:S(2)}, u32[]{:S(2)}) collective-permute-start(f32[32,4480]{1,0:T(8,128)} %get-tuple-element.34.both_ref), channel_id=1, source_target_pairs={{0,4},{4,8},{8,12},{12,16},{16,20},{20,24},{24,28},{1,5},{5,9},{9,... | collective-permute-start | bytes 1720328 | tf_op jit(solution)/shard_map/ppermute | solution.py:516
  9.8 1.1 %copy-start.2 = (f32[32,4480]{1,0:T(8,128)S(1)}, f32[32,4480]{1,0:T(8,128)}, u32[]{:S(2)}) copy-start(f32[32,4480]{1,0:T(8,128)} %get-tuple-element.34.both_ref) | copy-start | bytes 1720324
  10.8 19.5 %copy-start.3 = (f32[32,4480]{1,0:T(8,128)S(1)}, f32[32,4480]{1,0:T(8,128)}, u32[]{:S(2)}) copy-start(f32[32,4480]{1,0:T(8,128)} %get-tuple-element.34.both_ref) | copy-start | bytes 1720324
  15.8 26.8 %copy-start.1 = (f32[32,384]{1,0:T(8,128)S(1)}, f32[32,384]{1,0:T(8,128)}, u32[]{:S(2)}) copy-start(f32[32,384]{1,0:T(8,128)} %get-tuple-element.35.p_ref) | copy-start | bytes 147460
  17.8 10.6 %collective-permute-start.3 = (f32[32,1664]{1,0:T(8,128)S(1)}, f32[32,1664]{1,0:T(8,128)S(1)}, u32[]{:S(2)}, u32[]{:S(2)}) collective-permute-start(f32[32,1664]{1,0:T(8,128)S(1)} %get-tuple-element.44), channel_id=1, source_target_pairs={{0,8},{4,12},{8,16},{12,20},{1,9},{5,13},{9,17},{13,21},{2,10},{6,... | collective-permute-start | bytes 638984 | tf_op jit(solution)/shard_map/ppermute | solution.py:565
  19.1 23.4 %collective-permute-start.4 = (f32[32,1664]{1,0:T(8,128)S(1)}, f32[32,1664]{1,0:T(8,128)S(1)}, u32[]{:S(2)}, u32[]{:S(2)}) collective-permute-start(f32[32,1664]{1,0:T(8,128)S(1)} %get-tuple-element.45), channel_id=1, source_target_pairs={{4,8},{8,12},{12,16},{16,20},{5,9},{9,13},{13,17},{17,21},{6,10},{... | collective-permute-start | bytes 638984 | tf_op jit(solution)/shard_map/ppermute | solution.py:565
  20.4 22.1 %collective-permute-start.5 = (f32[32,1664]{1,0:T(8,128)S(1)}, f32[32,1664]{1,0:T(8,128)S(1)}, u32[]{:S(2)}, u32[]{:S(2)}) collective-permute-start(f32[32,1664]{1,0:T(8,128)S(1)} %get-tuple-element.46), channel_id=1, source_target_pairs={{12,8},{16,12},{20,16},{0,20},{13,9},{17,13},{21,17},{1,21},{14,10... | collective-permute-start | bytes 638984 | tf_op jit(solution)/shard_map/ppermute | solution.py:565
  24.4 18.2 %collective-permute-start.6 = (f32[32,1664]{1,0:T(8,128)S(1)}, f32[32,1664]{1,0:T(8,128)S(1)}, u32[]{:S(2)}, u32[]{:S(2)}) collective-permute-start(f32[32,1664]{1,0:T(8,128)S(1)} %get-tuple-element.47), channel_id=1, source_target_pairs={{16,8},{20,12},{0,16},{4,20},{17,9},{21,13},{1,17},{5,21},{18,10},... | collective-permute-start | bytes 638984 | tf_op jit(solution)/shard_map/ppermute | solution.py:565
  28.4 14.2 %collective-permute-start.7 = (f32[32,1664]{1,0:T(8,128)S(1)}, f32[32,1664]{1,0:T(8,128)S(1)}, u32[]{:S(2)}, u32[]{:S(2)}) collective-permute-start(f32[32,1664]{1,0:T(8,128)S(1)} %get-tuple-element.49), channel_id=1, source_target_pairs={{20,8},{0,12},{4,16},{8,20},{21,9},{1,13},{5,17},{9,21},{22,10},{2... | collective-permute-start | bytes 638984 | tf_op jit(solution)/shard_map/ppermute | solution.py:565
  40.6 14.1 %collective-permute-start.13 = (f32[32,4096]{1,0:T(8,128)S(1)}, f32[32,4096]{1,0:T(8,128)S(1)}, u32[]{:S(2)}, u32[]{:S(2)}) collective-permute-start(f32[32,4096]{1,0:T(8,128)S(1)} %get-tuple-element.42._), channel_id=1, source_target_pairs={{4,0},{8,4},{12,8},{16,12},{20,16},{24,20},{28,24},{5,1},{9,5},{13... | collective-permute-start | bytes 1572872 | tf_op jit(solution)/shard_map/ppermute | solution.py:516
  46.1 17.9 %collective-permute-start.8 = (f32[32,1024]{1,0:T(8,128)S(1)}, f32[32,1024]{1,0:T(8,128)S(1)}, u32[]{:S(2)}, u32[]{:S(2)}) collective-permute-start(f32[32,1024]{1,0:T(8,128)S(1)} %get-tuple-element.51), channel_id=1, source_target_pairs={{8,12},{12,16},{16,20},{20,24},{0,8},{9,13},{13,17},{17,21},{21,25... | collective-permute-start | bytes 393224 | tf_op jit(solution)/shard_map/ppermute | solution.py:587
  48.1 16.0 %collective-permute-start.9 = (f32[32,1024]{1,0:T(8,128)S(1)}, f32[32,1024]{1,0:T(8,128)S(1)}, u32[]{:S(2)}, u32[]{:S(2)}) collective-permute-start(f32[32,1024]{1,0:T(8,128)S(1)} %get-tuple-element.52), channel_id=1, source_target_pairs={{8,16},{12,20},{16,24},{20,28},{0,8},{9,17},{13,21},{17,25},{21,29... | collective-permute-start | bytes 393224 | tf_op jit(solution)/shard_map/ppermute | solution.py:587
  50.0 14.0 %collective-permute-start.10 = (f32[32,1024]{1,0:T(8,128)S(1)}, f32[32,1024]{1,0:T(8,128)S(1)}, u32[]{:S(2)}, u32[]{:S(2)}) collective-permute-start(f32[32,1024]{1,0:T(8,128)S(1)} %get-tuple-element.53), channel_id=1, source_target_pairs={{8,20},{12,24},{16,28},{20,12},{0,8},{9,21},{13,25},{17,29},{21,13... | collective-permute-start | bytes 393224 | tf_op jit(solution)/shard_map/ppermute | solution.py:587
  53.4 10.7 %collective-permute-start.11 = (f32[32,1024]{1,0:T(8,128)S(1)}, f32[32,1024]{1,0:T(8,128)S(1)}, u32[]{:S(2)}, u32[]{:S(2)}) collective-permute-start(f32[32,1024]{1,0:T(8,128)S(1)} %get-tuple-element.54), channel_id=1, source_target_pairs={{8,24},{12,28},{16,12},{20,16},{0,8},{9,25},{13,29},{17,13},{21,17... | collective-permute-start | bytes 393224 | tf_op jit(solution)/shard_map/ppermute | solution.py:587
  54.7 9.4 %collective-permute-start.12 = (f32[32,1024]{1,0:T(8,128)S(1)}, f32[32,1024]{1,0:T(8,128)S(1)}, u32[]{:S(2)}, u32[]{:S(2)}) collective-permute-start(f32[32,1024]{1,0:T(8,128)S(1)} %get-tuple-element.50.local_ref._), channel_id=1, source_target_pairs={{8,28},{9,29},{10,30},{11,31}} | collective-permute-start | bytes 393224 | tf_op jit(solution)/shard_map/ppermute | solution.py:587
  64.1 8.2 %collective-permute-start.16 = (f32[32,384]{1,0:T(8,128)S(1)}, f32[32,384]{1,0:T(8,128)S(1)}, u32[]{:S(2)}, u32[]{:S(2)}) collective-permute-start(f32[32,384]{1,0:T(8,128)S(1)} %get-tuple-element.61.refs_0_), channel_id=1, source_target_pairs={{0,3},{1,2},{2,1},{3,0},{4,7},{5,6},{6,5},{7,4},{8,11},{9,10},{10,... | collective-permute-start | bytes 147464 | tf_op jit(solution)/shard_map/ppermute | solution.py:522
  69.8 3.4 %collective-permute-start.15 = (f32[32,384]{1,0:T(8,128)S(1)}, f32[32,384]{1,0:T(8,128)S(1)}, u32[]{:S(2)}, u32[]{:S(2)}) collective-permute-start(f32[32,384]{1,0:T(8,128)S(1)} %get-tuple-element.61.refs_0_), channel_id=1, source_target_pairs={{0,2},{1,3},{2,0},{3,1},{4,6},{5,7},{6,4},{7,5},{8,10},{9,11},{10,... | collective-permute-start | bytes 147464 | tf_op jit(solution)/shard_map/ppermute | solution.py:522
  70.0 3.1 %collective-permute-start.14 = (f32[32,384]{1,0:T(8,128)S(1)}, f32[32,384]{1,0:T(8,128)S(1)}, u32[]{:S(2)}, u32[]{:S(2)}) collective-permute-start(f32[32,384]{1,0:T(8,128)S(1)} %get-tuple-element.61.refs_0_), channel_id=1, source_target_pairs={{0,1},{1,0},{2,3},{3,2},{4,5},{5,4},{6,7},{7,6},{8,9},{9,8},{10,11... | collective-permute-start | bytes 147464 | tf_op jit(solution)/shard_map/ppermute | solution.py:522
